TPU v7x, 32 devices: a whole 2x2x4 slice. The times are simulated.
32 devices in a mesh: dp: 8 (over z, y), seq: 4 (over x, core).
Axes of the slice: x: 2, y: 2, z: 4, core: 2. Of those that a mesh axis runs over, the one named last changes fastest.
Arguments:
- states: bfloat16 [8, 2560, 768], P('dp', 'seq'), may hold values from -6 to 6
- lengths: int32 [8], P('dp'), may hold values from 640 to 2560, as said below
- teacher: bfloat16 [8, 2560, 768], P('dp', 'seq'), may hold values from -6 to 6
- out_grad: bfloat16 [8, 2560, 768], P('dp', 'seq'), may hold values from -6 to 6
- q_weight: bfloat16 [768, 192], P('dp'), may hold values from -0.4375 to 0.4375
- k_weight: bfloat16 [768, 192], P('dp'), may hold values from -0.4375 to 0.4375
- v_weight: bfloat16 [768, 192], P('dp'), may hold values from -0.4375 to 0.4375
- q_bias: bfloat16 [768], P('dp'), may hold values from -0.59765625 to 0.59765625
- v_bias: bfloat16 [768], P('dp'), may hold values from -0.119628906 to 0.119628906
- o_weight: bfloat16 [768, 768], P('dp'), may hold values from -6 to 6
- o_bias: bfloat16 [768], P('dp'), may hold values from -0.59765625 to 0.59765625
- attn_gain: bfloat16 [768], P('dp'), may hold values from 0.5 to 1.5
- attn_bias: bfloat16 [768], P('dp'), may hold values from -0.59765625 to 0.59765625
- up_weight: bfloat16 [768, 768], P('dp'), may hold values from -0.4375 to 0.4375
- up_bias: bfloat16 [3072], P('dp'), may hold values from -0.59765625 to 0.59765625
- down_weight: bfloat16 [3072, 192], P('dp'), may hold values from -0.21875 to 0.21875
- down_bias: bfloat16 [768], P('dp'), may hold values from -0.59765625 to 0.59765625
- ffn_gain: bfloat16 [768], P('dp'), may hold values from 0.5 to 1.5
- ffn_bias: bfloat16 [768], P('dp'), may hold values from -0.59765625 to 0.59765625
Outputs:
- layer_out: bfloat16 [8, 2560, 768], P('dp', 'seq')
- loss_value: float32 [], replicated
- states_grad: bfloat16 [8, 2560, 768], P('dp', 'seq')
- grad_qw: float32 [768, 192], P('dp')
- grad_kw: float32 [768, 192], P('dp')
- grad_vw: float32 [768, 192], P('dp')
- grad_qb: float32 [768], P('dp')
- grad_vb: float32 [768], P('dp')
- grad_ow: float32 [768, 768], P('dp')
- grad_ob: float32 [768], P('dp')
- grad_ag: float32 [768], P('dp')
- grad_ab: float32 [768], P('dp')
- grad_uw: float32 [768, 768], P('dp')
- grad_ub: float32 [3072], P('dp')
- grad_dw: float32 [3072, 192], P('dp')
- grad_db: float32 [768], P('dp')
- grad_fg: float32 [768], P('dp')
- grad_fb: float32 [768], P('dp')
Inputs may be any that keep to these rules, and one draw needn't show every extreme that they name: `lengths`: every length is an integer from integers from 640 to 2560; some row has exactly 2560 and some other row exactly 640.
All inputs are finite; a program needn't handle non-finite values.
Results may differ from a plain program's by a relative error of at most 0.017.
Values may be sent and summed in bfloat16 or wider, within the bound.
A program may use at most 128 MiB of HBM per device.

v0:
```python
import jax
import jax.numpy as jnp
from jax import lax
from jax.sharding import PartitionSpec as P

HDIM = 64
GROUPS = 4
QBLK = 512


EPSILON = 1e-12
NEG_FILL = -1e30


def layer_norm(values, gain, shift):
    center = values - jnp.mean(values, axis=-1, keepdims=True)
    spread = jnp.mean(center * center, axis=-1, keepdims=True)
    return center * lax.rsqrt(spread + EPSILON) * gain + shift


def gelu_exact(values):
    return 0.5 * values * (1.0 + lax.erf(values * 0.7071067811865476))


def group_conv(values, weight, groups):
    tok_count, in_width = values.shape
    left_side = values.reshape(tok_count, groups, in_width // groups)
    right_side = weight.reshape(groups, in_width // groups, weight.shape[1])
    result = jnp.einsum("ngi,gio->ngo", left_side, right_side, preferred_element_type=jnp.float32)
    return result.reshape(tok_count, groups * weight.shape[1])


def group_back(grads, weight, groups):
    tok_count = grads.shape[0]
    right_side = weight.reshape(groups, weight.shape[0] // groups, weight.shape[1])
    left_side = grads.reshape(tok_count, groups, weight.shape[1])
    result = jnp.einsum("ngo,gio->ngi", left_side, right_side, preferred_element_type=jnp.float32)
    return result.reshape(tok_count, weight.shape[0])


def group_weight(values, grads, groups):
    tok_count, in_width = values.shape
    left_side = values.reshape(tok_count, groups, in_width // groups)
    right_side = grads.reshape(tok_count, groups, grads.shape[1] // groups)
    result = jnp.einsum("ngi,ngo->gio", left_side, right_side, preferred_element_type=jnp.float32)
    return result.reshape(in_width, grads.shape[1] // groups)


def head_forward(queries, keys_all, values, live):
    seq_len, head_dim = queries.shape
    factor = head_dim ** (-0.5)

    def block_step(query_block):
        scores = (
            jnp.einsum("qd,kd->qk", query_block, keys_all, preferred_element_type=jnp.float32)
            * factor
        )
        scores = jnp.where(live[None, :], scores, NEG_FILL)
        row_top = jnp.max(scores, axis=1, keepdims=True)
        weights = jnp.exp(scores - row_top)
        row_total = jnp.sum(weights, axis=1, keepdims=True)
        probs_low = (weights / row_total).astype(jnp.bfloat16)
        attended = jnp.dot(probs_low, values, preferred_element_type=jnp.float32)
        return (attended, (row_top + jnp.log(row_total))[:, 0])

    attended, log_sums = lax.map(block_step, queries.reshape(seq_len // QBLK, QBLK, head_dim))
    return (attended.reshape(seq_len, head_dim), log_sums.reshape(seq_len))


def head_backward(queries, keys_all, values, log_sums, grads, live):
    seq_len, head_dim = queries.shape
    factor = head_dim ** (-0.5)
    block_count = seq_len // QBLK

    def block_step(sums, block_items):
        key_sum, value_sum = sums
        query_block, lse_block, grad_block = block_items
        scores = (
            jnp.einsum("qd,kd->qk", query_block, keys_all, preferred_element_type=jnp.float32)
            * factor
        )
        scores = jnp.where(live[None, :], scores, NEG_FILL)
        probs = jnp.exp(scores - lse_block[:, None])
        value_sum = value_sum + jnp.einsum(
            "qk,qd->kd", probs.astype(jnp.bfloat16), grad_block, preferred_element_type=jnp.float32
        )
        prob_grad = jnp.einsum("qd,kd->qk", grad_block, values, preferred_element_type=jnp.float32)
        row_dot = jnp.sum(probs * prob_grad, axis=1, keepdims=True)
        score_low = (probs * (prob_grad - row_dot)).astype(jnp.bfloat16)
        query_grad = jnp.dot(score_low, keys_all, preferred_element_type=jnp.float32) * factor
        key_sum = (
            key_sum
            + jnp.einsum("qk,qd->kd", score_low, query_block, preferred_element_type=jnp.float32)
            * factor
        )
        return ((key_sum, value_sum), query_grad)

    zeros_kv = jnp.zeros((seq_len, head_dim), jnp.float32)
    (key_sum, value_sum), query_grad = lax.scan(
        block_step,
        (zeros_kv, zeros_kv),
        (
            queries.reshape(block_count, QBLK, head_dim),
            log_sums.reshape(block_count, QBLK),
            grads.reshape(block_count, QBLK, head_dim),
        ),
    )
    return (
        query_grad.reshape(seq_len, head_dim).astype(jnp.bfloat16),
        key_sum.astype(jnp.bfloat16),
        value_sum.astype(jnp.bfloat16),
    )


def row_attend(row_items):
    queries, keys_all, values, live = row_items

    def per_head(head_items):
        return head_forward(head_items[0], head_items[1], head_items[2], live)

    return lax.map(per_head, (queries, keys_all, values))


def row_backward(row_items):
    queries, keys_all, values, log_sums, grads, live = row_items

    def per_head(head_items):
        return head_backward(
            head_items[0], head_items[1], head_items[2], head_items[3], head_items[4], live
        )

    return lax.map(per_head, (queries, keys_all, values, log_sums, grads))


def local(
    states,
    lengths,
    teacher,
    out_grad,
    q_weight,
    k_weight,
    v_weight,
    q_bias,
    v_bias,
    o_weight,
    o_bias,
    attn_gain,
    attn_bias,
    up_weight,
    up_bias,
    down_weight,
    down_bias,
    ffn_gain,
    ffn_bias,
):
    gathered = (
        lax.all_gather(q_weight, "dp", axis=0, tiled=True),
        lax.all_gather(k_weight, "dp", axis=0, tiled=True),
        lax.all_gather(v_weight, "dp", axis=0, tiled=True),
        lax.all_gather(q_bias, "dp", axis=0, tiled=True),
        lax.all_gather(v_bias, "dp", axis=0, tiled=True),
        lax.all_gather(o_weight, "dp", axis=0, tiled=True),
        lax.all_gather(o_bias, "dp", axis=0, tiled=True),
        lax.all_gather(attn_gain, "dp", axis=0, tiled=True),
        lax.all_gather(attn_bias, "dp", axis=0, tiled=True),
        lax.all_gather(up_weight, "dp", axis=0, tiled=True),
        lax.all_gather(up_bias, "dp", axis=0, tiled=True),
        lax.all_gather(down_weight, "dp", axis=0, tiled=True),
        lax.all_gather(down_bias, "dp", axis=0, tiled=True),
        lax.all_gather(ffn_gain, "dp", axis=0, tiled=True),
        lax.all_gather(ffn_bias, "dp", axis=0, tiled=True),
    )
    (
        wq_all,
        wk_all,
        wv_all,
        bq_all,
        bv_all,
        wo_all,
        bo_all,
        ga_all,
        ba_all,
        wu_all,
        bu_all,
        wd_all,
        bd_all,
        gf_all,
        bf_all,
    ) = gathered
    row_count, piece_len, model_width = states.shape
    seq_count = lax.axis_size("seq")
    seq_index = lax.axis_index("seq")
    tok_count = row_count * piece_len
    seq_len = piece_len * seq_count
    head_width = model_width // seq_count
    local_heads = head_width // HDIM
    tokens = states.reshape(tok_count, model_width)
    slot_ids = jnp.arange(piece_len, dtype=jnp.int32) + seq_index * piece_len
    live_piece = (slot_ids[None, :] < lengths[:, None]).astype(jnp.float32).reshape(tok_count, 1)
    live_full = jnp.arange(seq_len, dtype=jnp.int32)[None, :] < lengths[:, None]

    def to_heads(flat):
        return flat.reshape(row_count, piece_len, seq_count, head_width)

    def head_major(grouped):
        return grouped.reshape(row_count, seq_len, local_heads, HDIM).transpose(0, 2, 1, 3)

    def back_layout(grouped):
        return grouped.transpose(0, 2, 1, 3).reshape(row_count, seq_len, 1, head_width)

    query_low = (group_conv(tokens, wq_all, GROUPS) + bq_all.astype(jnp.float32)).astype(
        jnp.bfloat16
    )
    key_low = group_conv(tokens, wk_all, GROUPS).astype(jnp.bfloat16)
    value_low = (group_conv(tokens, wv_all, GROUPS) + bv_all.astype(jnp.float32)).astype(
        jnp.bfloat16
    )
    queries_h, keys_h, values_h = (
        lax.all_to_all(to_heads(query_low), "seq", split_axis=2, concat_axis=1, tiled=True),
        lax.all_to_all(to_heads(key_low), "seq", split_axis=2, concat_axis=1, tiled=True),
        lax.all_to_all(to_heads(value_low), "seq", split_axis=2, concat_axis=1, tiled=True),
    )
    queries_h = head_major(queries_h)
    keys_h = head_major(keys_h)
    values_h = head_major(values_h)
    attended, log_sums = lax.map(row_attend, (queries_h, keys_h, values_h, live_full))
    context = lax.all_to_all(
        back_layout(attended.astype(jnp.bfloat16)), "seq", split_axis=1, concat_axis=2, tiled=True
    )
    context = context.reshape(tok_count, model_width)
    attn_out = jnp.dot(context, wo_all, preferred_element_type=jnp.float32) + bo_all.astype(
        jnp.float32
    )
    mid_pre = tokens.astype(jnp.float32) + attn_out
    gain_first = ga_all.astype(jnp.float32)
    shift_first = ba_all.astype(jnp.float32)
    first_out = layer_norm(mid_pre, gain_first, shift_first)
    first_low = first_out.astype(jnp.bfloat16)
    inner = group_conv(first_low, wu_all, GROUPS) + bu_all.astype(jnp.float32)
    act_low = gelu_exact(inner).astype(jnp.bfloat16)
    branch = group_conv(act_low, wd_all, GROUPS) + bd_all.astype(jnp.float32)
    final_pre = first_out + branch
    gain_final = gf_all.astype(jnp.float32)
    shift_final = bf_all.astype(jnp.float32)
    layer_full = layer_norm(final_pre, gain_final, shift_final)
    target = teacher.reshape(tok_count, model_width).astype(jnp.float32)
    errors = layer_full - target
    err_sum = jnp.sum(live_piece * errors * errors)
    live_sum = jnp.sum(live_piece)
    err_total, live_total = lax.psum((err_sum, live_sum), ("dp", "seq"))
    loss_value = err_total / (live_total * model_width)
    out_seed = live_piece * (
        out_grad.reshape(tok_count, model_width).astype(jnp.float32)
        + errors * (2.0 / (live_total * model_width))
    )
    unused, final_pull = jax.vjp(layer_norm, final_pre, gain_final, shift_final)
    grad_pre, grad_fg, grad_fb = final_pull(out_seed)
    branch_low = grad_pre.astype(jnp.bfloat16)
    grad_db = jnp.sum(branch_low.astype(jnp.float32), axis=0)
    grad_dw = group_weight(act_low, branch_low, GROUPS)
    grad_act = group_back(branch_low, wd_all, GROUPS)
    unused, gelu_pull = jax.vjp(gelu_exact, inner)
    inner_low = gelu_pull(grad_act)[0].astype(jnp.bfloat16)
    grad_ub = jnp.sum(inner_low.astype(jnp.float32), axis=0)
    grad_uw = group_weight(first_low, inner_low, GROUPS)
    grad_first = grad_pre + group_back(inner_low, wu_all, GROUPS)
    unused, first_pull = jax.vjp(layer_norm, mid_pre, gain_first, shift_first)
    grad_mid, grad_ag, grad_ab = first_pull(grad_first)
    attn_low = grad_mid.astype(jnp.bfloat16)
    grad_ob = jnp.sum(attn_low.astype(jnp.float32), axis=0)
    grad_ow = jnp.einsum("ni,no->io", context, attn_low, preferred_element_type=jnp.float32)
    context_grad = jnp.einsum(
        "no,io->ni", attn_low, wo_all, preferred_element_type=jnp.float32
    ).astype(jnp.bfloat16)
    grad_heads = head_major(
        lax.all_to_all(to_heads(context_grad), "seq", split_axis=2, concat_axis=1, tiled=True)
    )
    query_back, key_back, value_back = lax.map(
        row_backward, (queries_h, keys_h, values_h, log_sums, grad_heads, live_full)
    )
    query_flat, key_flat, value_flat = (
        lax.all_to_all(back_layout(query_back), "seq", split_axis=1, concat_axis=2, tiled=True),
        lax.all_to_all(back_layout(key_back), "seq", split_axis=1, concat_axis=2, tiled=True),
        lax.all_to_all(back_layout(value_back), "seq", split_axis=1, concat_axis=2, tiled=True),
    )
    query_flat = query_flat.reshape(tok_count, model_width)
    key_flat = key_flat.reshape(tok_count, model_width)
    value_flat = value_flat.reshape(tok_count, model_width)
    grad_qb = jnp.sum(query_flat.astype(jnp.float32), axis=0)
    grad_vb = jnp.sum(value_flat.astype(jnp.float32), axis=0)
    grad_qw = group_weight(tokens, query_flat, GROUPS)
    grad_kw = group_weight(tokens, key_flat, GROUPS)
    grad_vw = group_weight(tokens, value_flat, GROUPS)
    states_grad = (
        grad_mid
        + group_back(query_flat, wq_all, GROUPS)
        + group_back(key_flat, wk_all, GROUPS)
        + group_back(value_flat, wv_all, GROUPS)
    )
    states_grad = states_grad.astype(jnp.bfloat16).reshape(row_count, piece_len, model_width)
    partial_grads = (
        grad_qw,
        grad_kw,
        grad_vw,
        grad_qb,
        grad_vb,
        grad_ow,
        grad_ob,
        grad_ag,
        grad_ab,
        grad_uw,
        grad_ub,
        grad_dw,
        grad_db,
        grad_fg,
        grad_fb,
    )
    summed = (
        lax.psum(partial_grads[0].astype(jnp.bfloat16), "seq").astype(jnp.float32),
        lax.psum(partial_grads[1].astype(jnp.bfloat16), "seq").astype(jnp.float32),
        lax.psum(partial_grads[2].astype(jnp.bfloat16), "seq").astype(jnp.float32),
        lax.psum(partial_grads[3].astype(jnp.bfloat16), "seq").astype(jnp.float32),
        lax.psum(partial_grads[4].astype(jnp.bfloat16), "seq").astype(jnp.float32),
        lax.psum(partial_grads[5].astype(jnp.bfloat16), "seq").astype(jnp.float32),
        lax.psum(partial_grads[6].astype(jnp.bfloat16), "seq").astype(jnp.float32),
        lax.psum(partial_grads[7].astype(jnp.bfloat16), "seq").astype(jnp.float32),
        lax.psum(partial_grads[8].astype(jnp.bfloat16), "seq").astype(jnp.float32),
        lax.psum(partial_grads[9].astype(jnp.bfloat16), "seq").astype(jnp.float32),
        lax.psum(partial_grads[10].astype(jnp.bfloat16), "seq").astype(jnp.float32),
        lax.psum(partial_grads[11].astype(jnp.bfloat16), "seq").astype(jnp.float32),
        lax.psum(partial_grads[12].astype(jnp.bfloat16), "seq").astype(jnp.float32),
        lax.psum(partial_grads[13].astype(jnp.bfloat16), "seq").astype(jnp.float32),
        lax.psum(partial_grads[14].astype(jnp.bfloat16), "seq").astype(jnp.float32),
    )
    shares = (
        lax.psum_scatter(summed[0], "dp", scatter_dimension=0, tiled=True),
        lax.psum_scatter(summed[1], "dp", scatter_dimension=0, tiled=True),
        lax.psum_scatter(summed[2], "dp", scatter_dimension=0, tiled=True),
        lax.psum_scatter(summed[3], "dp", scatter_dimension=0, tiled=True),
        lax.psum_scatter(summed[4], "dp", scatter_dimension=0, tiled=True),
        lax.psum_scatter(summed[5], "dp", scatter_dimension=0, tiled=True),
        lax.psum_scatter(summed[6], "dp", scatter_dimension=0, tiled=True),
        lax.psum_scatter(summed[7], "dp", scatter_dimension=0, tiled=True),
        lax.psum_scatter(summed[8], "dp", scatter_dimension=0, tiled=True),
        lax.psum_scatter(summed[9], "dp", scatter_dimension=0, tiled=True),
        lax.psum_scatter(summed[10], "dp", scatter_dimension=0, tiled=True),
        lax.psum_scatter(summed[11], "dp", scatter_dimension=0, tiled=True),
        lax.psum_scatter(summed[12], "dp", scatter_dimension=0, tiled=True),
        lax.psum_scatter(summed[13], "dp", scatter_dimension=0, tiled=True),
        lax.psum_scatter(summed[14], "dp", scatter_dimension=0, tiled=True),
    )
    layer_out = layer_full.astype(jnp.bfloat16).reshape(row_count, piece_len, model_width)
    return (
        layer_out,
        loss_value,
        states_grad,
        shares[0],
        shares[1],
        shares[2],
        shares[3],
        shares[4],
        shares[5],
        shares[6],
        shares[7],
        shares[8],
        shares[9],
        shares[10],
        shares[11],
        shares[12],
        shares[13],
        shares[14],
    )


def solution(mesh):
    placed = (
        P("dp", "seq", None),
        P("dp"),
        P("dp", "seq", None),
        P("dp", "seq", None),
        P("dp", None),
        P("dp", None),
        P("dp", None),
        P("dp"),
        P("dp"),
        P("dp", None),
        P("dp"),
        P("dp"),
        P("dp"),
        P("dp", None),
        P("dp"),
        P("dp", None),
        P("dp"),
        P("dp"),
        P("dp"),
    )
    return jax.shard_map(
        local,
        mesh=mesh,
        in_specs=placed,
        out_specs=(
            P("dp", "seq", None),
            P(),
            P("dp", "seq", None),
            P("dp", None),
            P("dp", None),
            P("dp", None),
            P("dp"),
            P("dp"),
            P("dp", None),
            P("dp"),
            P("dp"),
            P("dp"),
            P("dp", None),
            P("dp"),
            P("dp", None),
            P("dp"),
            P("dp"),
            P("dp"),
        ),
        check_vma=False,
    )
```

profile of v0, /device:TPU:0, one launch (start us, length us, event | category | flops | bytes accessed | tf_op | source)
XLA Modules:
  0.0 1247.8 jit_solution(11840313325774664331)
XLA Ops:
  15.9 39.4 %all-reduce.18 = (bf16[768]{0:T(1024)(128)(2,1)S(1)}, bf16[768]{0:T(1024)(128)(2,1)S(1)}, bf16[768]{0:T(1024)(128)(2,1)}, bf16[768]{0:T(1024)(128)(2,1)}, bf16[7...) all-reduce(bf16[768]{0:T(1024)(128)(2,1)S(1)} %dynamic-update-slice, ...), channel_id=1, replica_groups=mesh['dp'=8,'seq'=4] {'dp'}, use_global_device_ids=true, to_apply=%add | all-reduce | flops 6144 | bytes 24576
  55.4 31.2 %all_gather.48 = bf16[768,192]{1,0:T(8,128)(2,1)S(1)} all-gather(bf16[96,192]{1,0:T(8,128)(2,1)} %param.33), channel_id=1, replica_groups=mesh['dp'=8,'seq'=4] {'dp'}, dimensions={0}, use_global_device_ids=true | all-gather | bytes 331776 | tf_op jit(solution)/shard_map/all_gather | solution.py:159
  94.2 31.3 %all_gather.45 = bf16[768,192]{1,0:T(8,128)(2,1)S(1)} all-gather(bf16[96,192]{1,0:T(8,128)(2,1)S(1)} %copy-done.32), channel_id=1, replica_groups=mesh['dp'=8,'seq'=4] {'dp'}, dimensions={0}, use_global_device_ids=true | all-gather | bytes 331776 | tf_op jit(solution)/shard_map/all_gather | solution.py:157
  131.3 31.2 %all_gather.47 = bf16[768,192]{1,0:T(8,128)(2,1)S(1)} all-gather(bf16[96,192]{1,0:T(8,128)(2,1)S(1)} %copy-done.33), channel_id=1, replica_groups=mesh['dp'=8,'seq'=4] {'dp'}, dimensions={0}, use_global_device_ids=true | all-gather | bytes 331776 | tf_op jit(solution)/shard_map/all_gather | solution.py:158
  188.1 75.8 %while.78 = (s32[]{:T(128)}, bf16[3,2560,64]{1,2,0:T(8,128)(2,1)}, f32[3,2560]{1,0:T(4,128)S(1)}, bf16[3,2560,64]{2,1,0:T(8,128)(2,1)S(1)}, bf16[3,2560,64]{2,1,...) while((s32[]{:T(128)}, bf16[3,2560,64]{1,2,0:T(8,128)(2,1)}, ...), condition=%wide.region_5.6_spmd.clone, body=%wide.region_0.5_spmd.clone.sunk | while | flops 346032128 | bytes 22284132 | solution.py:121
  191.1 19.8 %while.81 = (s32[]{:T(128)}, bf16[5,512,64]{1,2,0:T(8,128)(2,1)}, f32[5,512]{1,0:T(8,128)S(1)}, pred[2560]{0:T(1024)(128)(4,1)S(1)}, bf16[5,512,64]{2,1,0:T(8,12...) while((s32[]{:T(128)}, bf16[5,512,64]{1,2,0:T(8,128)(2,1)}, ...), condition=%wide.region_4.4_spmd, body=%wide.region_1.3_spmd.sunk | while | flops 346029568 | bytes 18308236 | solution.py:66
  216.4 19.8 %while.81 = (s32[]{:T(128)}, bf16[5,512,64]{1,2,0:T(8,128)(2,1)}, f32[5,512]{1,0:T(8,128)S(1)}, pred[2560]{0:T(1024)(128)(4,1)S(1)}, bf16[5,512,64]{2,1,0:T(8,12...) while((s32[]{:T(128)}, bf16[5,512,64]{1,2,0:T(8,128)(2,1)}, ...), condition=%wide.region_4.4_spmd, body=%wide.region_1.3_spmd.sunk | while | flops 346029568 | bytes 18308236 | solution.py:66
  241.6 19.8 %while.81 = (s32[]{:T(128)}, bf16[5,512,64]{1,2,0:T(8,128)(2,1)}, f32[5,512]{1,0:T(8,128)S(1)}, pred[2560]{0:T(1024)(128)(4,1)S(1)}, bf16[5,512,64]{2,1,0:T(8,12...) while((s32[]{:T(128)}, bf16[5,512,64]{1,2,0:T(8,128)(2,1)}, ...), condition=%wide.region_4.4_spmd, body=%wide.region_1.3_spmd.sunk | while | flops 346029568 | bytes 18308236 | solution.py:66
  294.6 44.6 %psum.120 = f32[]{:T(128)} all-reduce(f32[]{:T(128)} %fusion.63), channel_id=1, replica_groups=mesh['dp'=8,'seq'=4] {'dp','seq'}, use_global_device_ids=true, to_apply=%region_13.14 | all-reduce | flops 1 | bytes 8 | tf_op jit(solution)/shard_map/psum | solution.py:250
  339.3 25.9 %all-gather = bf16[8,1,384]{2,1,0:T(2,128)(2,1)S(1)} all-gather(bf16[1,1,384]{2,1,0:T(2,128)(2,1)S(1)} %reshape.404), channel_id=1, replica_groups=mesh['dp'=8,'seq'=4] {'dp'}, dimensions={0}, use_global_device_ids=true | all-gather | bytes 6912 | tf_op jit(solution)/shard_map/all_gather | solution.py:167
  457.6 143.2 %while.80 = (s32[]{:T(128)}, bf16[3,2560,64]{1,2,0:T(8,128)(2,1)}, bf16[3,2560,64]{1,2,0:T(8,128)(2,1)}, bf16[3,2560,64]{1,2,0:T(8,128)(2,1)}, bf16[3,2560,64]{2...) while((s32[]{:T(128)}, bf16[3,2560,64]{1,2,0:T(8,128)(2,1)}, ...), condition=%wide.region_22.23_spmd.clone, body=%wide.region_18.22_spmd.clone.sunk | while | flops 851838976 | bytes 51175344 | solution.py:132
  462.9 38.6 %while.82 = (s32[]{:T(128)}, f32[2560,64]{0,1:T(8,128)S(1)}, f32[2560,64]{0,1:T(8,128)S(1)}, bf16[5,512,64]{1,2,0:T(8,128)(2,1)}, pred[2560]{0:T(1024)(128)(4,1)...) while((s32[]{:T(128)}, f32[2560,64]{0,1:T(8,128)S(1)}, ...), condition=%wide.region_21.21_spmd.clone, body=%wide.region_19.20_spmd.clone.sunk | while | flops 851508736 | bytes 43922588 | solution.py:99
  510.6 38.6 %while.82 = (s32[]{:T(128)}, f32[2560,64]{0,1:T(8,128)S(1)}, f32[2560,64]{0,1:T(8,128)S(1)}, bf16[5,512,64]{1,2,0:T(8,128)(2,1)}, pred[2560]{0:T(1024)(128)(4,1)...) while((s32[]{:T(128)}, f32[2560,64]{0,1:T(8,128)S(1)}, ...), condition=%wide.region_21.21_spmd.clone, body=%wide.region_19.20_spmd.clone.sunk | while | flops 851508736 | bytes 43922588 | solution.py:99
  558.4 38.6 %while.82 = (s32[]{:T(128)}, f32[2560,64]{0,1:T(8,128)S(1)}, f32[2560,64]{0,1:T(8,128)S(1)}, bf16[5,512,64]{1,2,0:T(8,128)(2,1)}, pred[2560]{0:T(1024)(128)(4,1)...) while((s32[]{:T(128)}, f32[2560,64]{0,1:T(8,128)S(1)}, ...), condition=%wide.region_21.21_spmd.clone, body=%wide.region_19.20_spmd.clone.sunk | while | flops 851508736 | bytes 43922588 | solution.py:99
  606.5 15.5 %reduce.18 = bf16[2560,192]{1,0:T(8,128)(2,1)} reduce(bf16[2560,1,1,192]{3,2,1,0:T(2,128)(2,1)S(1)} %bitcast.340, bf16[]{:T(256)} %broadcast.277), dimensions={1,2}, to_apply=%bitcast.225.reduce_sub_computation | reduce | bytes 1966082
  636.3 15.5 %reduce.16 = bf16[2560,192]{1,0:T(8,128)(2,1)} reduce(bf16[2560,1,1,192]{3,2,1,0:T(2,128)(2,1)S(1)} %bitcast.341, bf16[]{:T(256)} %broadcast.277), dimensions={1,2}, to_apply=%bitcast.221.reduce_sub_computation | reduce | bytes 1966082
  673.0 15.4 %reduce.17 = bf16[2560,192]{1,0:T(8,128)(2,1)} reduce(bf16[2560,1,1,192]{3,2,1,0:T(2,128)(2,1)S(1)} %bitcast.339, bf16[]{:T(256)} %broadcast.277), dimensions={1,2}, to_apply=%bitcast.223.reduce_sub_computation | reduce | bytes 1966082
  729.6 94.9 %all-reduce.23.cloned.1.call-done = (bf16[768,192]{1,0:T(8,128)(2,1)}, bf16[768,192]{1,0:T(8,128)(2,1)}, bf16[768,192]{1,0:T(8,128)(2,1)}, bf16[768,768]{1,0:T(8...) async-done(((bf16[768,192]{1,0:T(8,128)(2,1)}, bf16[768,192]{1,0:T(8,128)(2,1)}, bf16[768,192]{1,0:T(8,128)(2,1)}, bf16[768,768]{1,0:T(8,128)(2,1)}, ...) | async-done | bytes 4423696 | tf_op jit(solution)/shard_map/psum | solution.py:319
  838.9 39.9 %psum.119 = f32[]{:T(128)} all-reduce(f32[]{:T(128)} %get-tuple-element.411), channel_id=1, replica_groups=mesh['dp'=8,'seq'=4] {'dp','seq'}, use_global_device_ids=true, to_apply=%region_11.12 | all-reduce | flops 1 | bytes 8 | tf_op jit(solution)/shard_map/psum | solution.py:250
  896.2 36.5 %all-reduce.17 = (f32[768]{0:T(1024)S(1)}, f32[768]{0:T(1024)S(1)}, f32[768]{0:T(1024)S(1)}, f32[768]{0:T(1024)S(1)}, f32[768]{0:T(1024)S(1)}, /*index=5*/f32[30...) all-reduce(bf16[768]{0:T(1024)(128)(2,1)S(1)} %get-tuple-element.49, ...), channel_id=5, replica_groups=mesh['dp'=8,'seq'=4] {'dp'}, use_global_device_ids=true, to_apply=%region_31.32.clone | all-reduce | flops 9216 | bytes 55296
  956.6 65.4 %reduce-scatter.11.cloned.1.call-done = f32[96,192]{1,0:T(8,128)} async-done(((f32[768,192]{1,0:T(8,128)}), f32[96,192]{1,0:T(8,128)}) %reduce-scatter.11.cloned.1.call-update) | async-done | bytes 73744 | tf_op jit(solution)/shard_map/reduce_scatter | solution.py:338
  1022.0 72.4 %reduce-scatter.13.cloned.1.call-done = f32[96,768]{1,0:T(8,128)} async-done(((f32[768,768]{1,0:T(8,128)}), f32[96,768]{1,0:T(8,128)}) %reduce-scatter.13.cloned.1.call-update) | async-done | bytes 294928 | tf_op jit(solution)/shard_map/reduce_scatter | solution.py:341
  1094.4 72.5 %reduce-scatter.15.cloned.1.call-done = f32[96,768]{1,0:T(8,128)} async-done(((f32[768,768]{1,0:T(8,128)}), f32[96,768]{1,0:T(8,128)}) %reduce-scatter.15.cloned.1.call-update) | async-done | bytes 294928 | tf_op jit(solution)/shard_map/reduce_scatter | solution.py:345
  1167.0 72.4 %reduce-scatter.17.cloned.1.call-done = f32[384,192]{0,1:T(8,128)} async-done(((f32[3072,192]{0,1:T(8,128)}), f32[384,192]{0,1:T(8,128)}) %reduce-scatter.17.cloned.1.call-update) | async-done | bytes 294928 | tf_op jit(solution)/shard_map/reduce_scatter | solution.py:347
  (564 shorter events, 521.6 us)
Async XLA Ops:
  88.3 74.1 %copy-start = (bf16[1,640,768]{1,2,0:T(8,128)(2,1)}, bf16[1,640,768]{1,2,0:T(8,128)(2,1)S(1)}, u32[]{:S(2)}) copy-start(bf16[1,640,768]{1,2,0:T(8,128)(2,1)S(1)} %copy.158) | copy-start | bytes 2949124
  89.8 37.9 %all-to-all-start.2 = ((bf16[1,640,4,192]{1,3,0,2:T(8,128)(2,1)}), bf16[1,640,4,192]{1,3,0,2:T(8,128)(2,1)S(1)}, u32[]{:S(2)}, u32[]{:S(2)}) async-start(bf16[1,640,4,192]{1,3,0,2:T(8,128)(2,1)} %fusion.43), calls=%async_computation.2 | async-start | bytes 1966080 | tf_op jit(solution)/shard_map/all_to_all | solution.py:221
  93.4 284.1 %all-gather.5.cloned.1.call-start = ((), (), s32[]{:S(2)}) async-start(), calls=%async_computation.14 | async-start | bytes 1327104 | tf_op jit(solution)/shard_map/all_gather | solution.py:162
  127.7 37.0 %all-to-all-start = ((bf16[1,640,4,192]{1,3,0,2:T(8,128)(2,1)}), bf16[1,640,4,192]{1,3,0,2:T(8,128)(2,1)S(1)}, u32[]{:S(2)}, u32[]{:S(2)}) async-start(bf16[1,640,4,192]{1,3,0,2:T(8,128)(2,1)} %fusion.42), calls=%async_computation | async-start | bytes 1966080 | tf_op jit(solution)/shard_map/all_to_all | solution.py:219
  165.6 17.2 %all-to-all-start.1 = ((bf16[1,640,4,192]{1,3,0,2:T(8,128)(2,1)}), bf16[1,640,4,192]{1,3,0,2:T(8,128)(2,1)S(1)}, u32[]{:S(2)}, u32[]{:S(2)}) async-start(bf16[1,640,4,192]{1,3,0,2:T(8,128)(2,1)} %fusion.41), calls=%async_computation.1 | async-start | bytes 1966080 | tf_op jit(solution)/shard_map/all_to_all | solution.py:220
  169.2 214.2 %all-gather.7.cloned.1.call-start = ((), (), s32[]{:S(2)}) async-start(), calls=%async_computation.15 | async-start | bytes 1327104 | tf_op jit(solution)/shard_map/all_gather | solution.py:166
  286.4 52.8 %copy-start.46 = (bf16[768]{0:T(1024)(128)(2,1)S(1)}, bf16[768]{0:T(1024)(128)(2,1)}, u32[]{:S(2)}) copy-start(bf16[768]{0:T(1024)(128)(2,1)} %get-tuple-element.498) | copy-start | bytes 4612
  286.4 52.8 %copy-start.45 = (bf16[768]{0:T(1024)(128)(2,1)S(1)}, bf16[768]{0:T(1024)(128)(2,1)}, u32[]{:S(2)}) copy-start(bf16[768]{0:T(1024)(128)(2,1)} %get-tuple-element.493) | copy-start | bytes 4612
  286.4 52.9 %copy-start.44 = (bf16[768]{0:T(1024)(128)(2,1)S(1)}, bf16[768]{0:T(1024)(128)(2,1)}, u32[]{:S(2)}) copy-start(bf16[768]{0:T(1024)(128)(2,1)} %get-tuple-element.496) | copy-start | bytes 4612
  286.4 52.9 %copy-start.43 = (bf16[768]{0:T(1024)(128)(2,1)S(1)}, bf16[768]{0:T(1024)(128)(2,1)}, u32[]{:S(2)}) copy-start(bf16[768]{0:T(1024)(128)(2,1)} %get-tuple-element.497) | copy-start | bytes 4612
  289.0 77.0 %all-to-all-start.3 = ((bf16[4,2,61440]{2,1,0:T(2,128)(2,1)}), bf16[4,2,61440]{2,1,0:T(2,128)(2,1)}, u32[]{:S(2)}, u32[]{:S(2)}) async-start(bf16[4,2,61440]{2,1,0:T(2,128)(2,1)} %reshape.442), calls=%async_computation.3 | async-start | bytes 1966080 | tf_op jit(solution)/shard_map/all_to_all | solution.py:227
  293.3 99.6 %all-gather.9.cloned.1.call-start = ((), (), s32[]{:S(2)}) async-start(), calls=%async_computation.16 | async-start | bytes 1327104 | tf_op jit(solution)/shard_map/all_gather | solution.py:168
  438.1 17.3 %all-to-all-start.4 = ((bf16[1,640,4,192]{1,3,0,2:T(8,128)(2,1)}), bf16[1,640,4,192]{1,3,0,2:T(8,128)(2,1)S(1)}, u32[]{:S(2)}, u32[]{:S(2)}) async-start(bf16[1,640,4,192]{1,3,0,2:T(8,128)(2,1)} %bitcast.50), calls=%async_computation.4 | async-start | bytes 1966080 | tf_op jit(solution)/shard_map/all_to_all | solution.py:276
  626.1 29.9 %all-to-all-start.5 = ((bf16[4,2,61440]{2,1,0:T(2,128)(2,1)}), bf16[4,2,61440]{2,1,0:T(2,128)(2,1)}, u32[]{:S(2)}, u32[]{:S(2)}) async-start(bf16[4,2,61440]{2,1,0:T(2,128)(2,1)} %reshape.448), calls=%async_computation.5 | async-start | bytes 1966080 | tf_op jit(solution)/shard_map/all_to_all | solution.py:282
  656.0 36.7 %all-to-all-start.7 = ((bf16[4,2,61440]{2,1,0:T(2,128)(2,1)}), bf16[4,2,61440]{2,1,0:T(2,128)(2,1)}, u32[]{:S(2)}, u32[]{:S(2)}) async-start(bf16[4,2,61440]{2,1,0:T(2,128)(2,1)} %reshape.444), calls=%async_computation.7 | async-start | bytes 1966080 | tf_op jit(solution)/shard_map/all_to_all | solution.py:284
  692.7 24.6 %all-to-all-start.6 = ((bf16[4,2,61440]{2,1,0:T(2,128)(2,1)}), bf16[4,2,61440]{2,1,0:T(2,128)(2,1)}, u32[]{:S(2)}, u32[]{:S(2)}) async-start(bf16[4,2,61440]{2,1,0:T(2,128)(2,1)} %reshape.446), calls=%async_computation.6 | async-start | bytes 1966080 | tf_op jit(solution)/shard_map/all_to_all | solution.py:283
  696.9 127.6 %all-reduce.23.cloned.1.call-start = ((), (), s32[]{:S(2)}) async-start(), calls=%async_computation.23 | async-start | bytes 9437184 | tf_op jit(solution)/shard_map/psum | solution.py:319
  729.6 222.1 %reduce-scatter.7.cloned.1.call-start = ((), (), s32[]{:S(2)}) async-start(), calls=%async_computation.17 | async-start | bytes 884736 | tf_op jit(solution)/shard_map/reduce_scatter | solution.py:336
  826.5 130.0 %reduce-scatter.9.cloned.1.call-start = ((), (), s32[]{:S(2)}) async-start(), calls=%async_computation.18 | async-start | bytes 884736 | tf_op jit(solution)/shard_map/reduce_scatter | solution.py:337
  827.6 194.4 %reduce-scatter.11.cloned.1.call-start = ((), (), s32[]{:S(2)}) async-start(), calls=%async_computation.19 | async-start | bytes 884736 | tf_op jit(solution)/shard_map/reduce_scatter | solution.py:338
  828.6 265.9 %reduce-scatter.13.cloned.1.call-start = ((), (), s32[]{:S(2)}) async-start(), calls=%async_computation.20 | async-start | bytes 2654208 | tf_op jit(solution)/shard_map/reduce_scatter | solution.py:341
  831.5 335.5 %reduce-scatter.15.cloned.1.call-start = ((), (), s32[]{:S(2)}) async-start(), calls=%async_computation.21 | async-start | bytes 2654208 | tf_op jit(solution)/shard_map/reduce_scatter | solution.py:345
  834.4 404.9 %reduce-scatter.17.cloned.1.call-start = ((), (), s32[]{:S(2)}) async-start(), calls=%async_computation.22 | async-start | bytes 2654208 | tf_op jit(solution)/shard_map/reduce_scatter | solution.py:347
  881.6 55.8 %copy-start.19 = (bf16[768,192]{1,0:T(8,128)(2,1)S(1)}, bf16[768,192]{1,0:T(8,128)(2,1)}, u32[]{:S(2)}) copy-start(bf16[768,192]{1,0:T(8,128)(2,1)} %copy-done.18) | copy-start | bytes 884740
  (59 other events, 416.4 us)
Sparse Core Ops, SparseCore 0:
  96.4 39.5 all-gather.4
  172.2 38.9 all-gather.6
  296.2 39.1 all-gather.8
  729.7 94.7 all-reduce.22
  828.2 62.7 reduce-scatter.6
  895.0 61.4 reduce-scatter.8
  960.5 61.5 reduce-scatter.10
  1026.5 67.8 reduce-scatter.12
  1098.9 68.0 reduce-scatter.14
  1171.3 68.0 reduce-scatter.16
where the time goes:
time: 1260 us; the launch traced here: 1250 us
  waiting for transfers between devices  400 us (32%)
  blocking collectives  291 us (23%)
  matrix products  195 us (15%)
  local copies, waits for them, and re-layouts  181 us (14%)
  other arithmetic  127 us (10%)
  starting transfers between devices  31.7 us (3%)
  between operations  20.5 us (2%)
    psum x1, waiting for transfers between devices, local(): lax.psum(partial_grads[0].astype(jnp.bfloat16), 'seq').astype(jnp.float32)  94.9 us
    psum x2, blocking collectives, local(): err_total, live_total = lax.psum((err_sum, live_sum), ('dp', 'seq'))  84.4 us
    unnamed x2, blocking collectives  76 us
    reduce_scatter x1, waiting for transfers between devices, local(): lax.psum_scatter(summed[9], 'dp', scatter_dimension=0, tiled=True)  72.5 us
    reduce_scatter x1, waiting for transfers between devices, local(): lax.psum_scatter(summed[5], 'dp', scatter_dimension=0, tiled=True)  72.4 us
    reduce_scatter x1, waiting for transfers between devices, local(): lax.psum_scatter(summed[11], 'dp', scatter_dimension=0, tiled=True)  72.4 us
    unnamed x143, local copies, waits for them, and re-layouts  71.6 us
    reduce_scatter x1, waiting for transfers between devices, local(): lax.psum_scatter(summed[2], 'dp', scatter_dimension=0, tiled=True)  65.4 us
  transfers between devices with their start and end apart: 18, of which 8 were waited for; matrix products, arithmetic and copies ran while one was open for 20% of the time, Pallas kernels for 0%

commit v1 on v0

v1 whole, which is shorter than its diff:
```python
import functools
import math

import jax
import jax.numpy as jnp
from jax import lax
from jax.experimental import pallas as pl
from jax.experimental.pallas import tpu as pltpu
from jax.sharding import PartitionSpec as P

HDIM = 64
GROUPS = 4
EPSILON = 1e-12
NEG_FILL = -1e30
LANES = 128
AUG = 16
LOG2E = 1.4426950408889634
MESH = pl.DeviceIdType.MESH
F32 = jnp.float32
BF16 = jnp.bfloat16
VMEM_LIMIT = 60 * 1024 * 1024


def mm(left, right, left_dim, right_dim):
    return lax.dot_general(
        left, right, (((left_dim,), (right_dim,)), ((), ())), preferred_element_type=F32
    )


def iota(shape, dim):
    return lax.broadcasted_iota(jnp.int32, shape, dim)


def remote(src, dst, send_sem, recv_sem, **where):
    return pltpu.make_async_remote_copy(
        src_ref=src,
        dst_ref=dst,
        send_sem=send_sem,
        recv_sem=recv_sem,
        device_id=where,
        device_id_type=MESH,
    )


def three_parts(row):
    high = row.astype(BF16)
    rest = row - high.astype(F32)
    middle = rest.astype(BF16)
    low = (rest - middle.astype(F32)).astype(BF16)
    return high, middle, low


def greet(cfg, me, my_dp, with_dp):
    barrier = pltpu.get_barrier_semaphore()
    count = cfg.seq - 1
    for d in range(1, cfg.seq):
        pl.semaphore_signal(barrier, inc=1, device_id={"seq": me ^ d}, device_id_type=MESH)
    if with_dp:
        count += cfg.dp - 1
        for e in range(1, cfg.dp):
            pl.semaphore_signal(
                barrier, inc=1, device_id={"dp": lax.rem(my_dp + e, cfg.dp)}, device_id_type=MESH
            )
    pl.semaphore_wait(barrier, count)


class Config:
    def __init__(self, dp, seq, piece, width, hidden, shard):
        self.dp, self.seq, self.piece, self.width, self.hidden, self.shard = (
            dp,
            seq,
            piece,
            width,
            hidden,
            shard,
        )
        self.slots = piece * seq
        self.group = width // GROUPS
        self.heads = self.group // HDIM
        self.per_group = dp // GROUPS
        self.split = shard % 32 == 0 and seq == 4
        self.half = shard // 2
        self.quarter = hidden // dp // 4


def attend_kernel(cfg, row, *refs):
    split = cfg.split
    refs = list(refs)
    take = lambda n: [refs.pop(0) for _ in range(n)]
    if split:
        states, small, wq, wk, wv, ow, uw, dw = take(8)
    else:
        states, smalls, wgroup_in = take(3)
    context_r, q_t, k_n, v_n, context_s, x_group, x_own, w_group = take(8)
    if split:
        smalls, gath_ou, gath_d = take(3)
    v_t, scores0, scores1, w_pad = take(4)
    a_send, a_recv, c_send, c_recv = take(4)
    if split:
        w_recv, s_send, s_recv, w_send_sem, w_recv_sem, own_sem = take(6)
        p_send, p_recv, x_send, x_recv, y_send, y_recv, z_send, z_recv = take(8)
    me = lax.axis_index("seq")
    my_dp = lax.axis_index("dp")
    piece, width, group, heads, seq = cfg.piece, cfg.width, cfg.group, cfg.heads, cfg.seq
    slots, shard, n_dp = cfg.slots, cfg.shard, cfg.dp
    order = [d for d in range(seq - 1, -1, -1)]

    for g in range(GROUPS):
        for c in range(0, group, 64):
            x_own[g, c : c + 64, :] = states[:, g * group + c : g * group + c + 64].T

    greet(cfg, me, my_dp, split)

    x_copies = {}
    for d in order[:-1]:
        x_copies[d] = remote(
            x_own.at[me ^ d],
            x_group.at[me, pl.ds(0, group)],
            a_send.at[d],
            a_recv.at[d],
            seq=me ^ d,
        )
        x_copies[d].start()

    if split:
        kinds = (wq, wk, wv)
        my_slot = lax.rem(my_dp, cfg.per_group)
        holder = my_dp // cfg.per_group == me

        def w_copy(kind, e):
            return remote(
                kinds[kind],
                w_recv.at[my_slot, kind],
                w_send_sem.at[e, kind],
                w_recv_sem.at[my_slot, kind],
                dp=lax.rem(my_dp + e, n_dp),
            )

        @pl.when(holder)
        def _():
            for e in range(1, n_dp):
                for kind in range(3):
                    w_copy(kind, e).start()

        s_copies = []
        for e in range(1, n_dp):
            s_copies.append(
                remote(
                    small,
                    smalls.at[my_dp],
                    s_send.at[e],
                    s_recv.at[e],
                    dp=lax.rem(my_dp + e, n_dp),
                )
            )
            s_copies[-1].start()

        xbit, core = me // 2, lax.rem(me, 2)
        half_rows = pl.ds(pl.multiple_of(core * cfg.half, 16), cfg.half)
        quarter_rows = pl.ds(pl.multiple_of(me * cfg.quarter, 16), cfg.quarter)

        def p_pair(e, src):
            target = lax.rem(my_dp + e, n_dp)
            return (
                remote(
                    src.at[half_rows],
                    gath_ou.at[xbit, my_dp, core],
                    p_send.at[e, 0],
                    p_recv.at[e, 0],
                    dp=target,
                ),
                remote(
                    dw.at[quarter_rows],
                    gath_d.at[my_dp, me],
                    p_send.at[e, 1],
                    p_recv.at[e, 1],
                    dp=target,
                ),
            )

        for e in range(1, n_dp):

            @pl.when(xbit == 0)
            def _():
                p_pair(e, ow)[0].start()

            @pl.when(xbit == 1)
            def _():
                p_pair(e, uw)[0].start()

            p_pair(e, ow)[1].start()

        smalls[my_dp] = small[...]
        for x, src in enumerate((ow, uw)):
            for c in range(2):
                gath_ou[x, my_dp, c] = src[c * cfg.half : (c + 1) * cfg.half]
        for q in range(4):
            gath_d[my_dp, q] = dw[q * cfg.quarter : (q + 1) * cfg.quarter]

        @pl.when(holder)
        def _():
            for kind in range(3):
                w_recv[my_slot, kind] = kinds[kind][...]

    x_group[me, 0:group] = x_own[me]

    if split:
        for e in range(1, n_dp):
            s_copies[e - 1].wait_recv()
        for t in range(cfg.per_group):

            @pl.when(me * cfg.per_group + t != my_dp)
            def _():
                for kind in range(3):
                    remote(
                        kinds[kind],
                        w_recv.at[t, kind],
                        w_send_sem.at[0, kind],
                        w_recv_sem.at[t, kind],
                        dp=my_dp,
                    ).wait_recv()

            for kind in range(3):
                w_group[kind, t * shard : (t + 1) * shard] = w_recv[t, kind]
    else:
        for kind in range(3):
            w_group[kind] = wgroup_in[kind]

    cols = heads * LANES
    lane = iota((group, cols), 1)
    spread = jnp.where(
        (((lane >> 7) * HDIM + (lane & 127)) == iota((group, cols), 0)) & ((lane & 127) < HDIM),
        1.0,
        0.0,
    ).astype(BF16)
    for kind in range(3):
        w_pad[kind, 0:group] = mm(w_group[kind], spread, 1, 0).astype(BF16)
    vec_rows = jnp.zeros((AUG, cols), F32)
    lane = iota((LANES, cols), 1)
    source = iota((LANES, cols), 0)
    for t in range(cfg.per_group):
        spread = jnp.where(
            (((lane >> 7) * HDIM + (lane & 127)) == source + t * shard)
            & ((lane & 127) < HDIM)
            & (source < shard),
            1.0,
            0.0,
        ).astype(BF16)
        vec_rows += mm(smalls[me * cfg.per_group + t].astype(BF16), spread, 1, 0)
    row_id = iota((AUG, cols), 0)
    lane = iota((AUG, cols), 1) & 127
    zero = jnp.zeros((AUG, cols), F32)
    first = row_id == 0
    w_pad[0, group : group + AUG] = jnp.where(first, vec_rows[0:1], zero).astype(BF16)
    ones_k = (first & (lane > HDIM) & (lane <= HDIM + 3)) | ((row_id == 1) & (lane == HDIM))
    w_pad[1, group : group + AUG] = jnp.where(ones_k, 1.0, zero).astype(BF16)
    ones_v = (lane >= HDIM) & (lane < HDIM + 3)
    w_pad[2, group : group + AUG] = jnp.where(
        first, jnp.where(ones_v, 1.0, vec_rows[1:2]), zero
    ).astype(BF16)

    length = smalls[my_dp, 12 + row : 13 + row, 0:1]
    aug_row = iota((AUG, piece), 0)
    q_rows = jnp.where(iota((HDIM, piece), 0) == 0, 1.0, 0.0).astype(BF16)
    factor = LOG2E * HDIM**-0.5

    def project(t):
        slot = (iota((AUG, piece), 1) + t * piece).astype(F32)
        mask = jnp.where(slot < length, 0.0, NEG_FILL)
        x_group[t, group : group + AUG] = jnp.where(
            aug_row == 0, 1.0, jnp.where(aug_row == 1, mask, 0.0)
        ).astype(BF16)
        x = x_group[t]
        queries = mm(w_pad[0], x, 0, 0) * factor
        values = mm(w_pad[2], x, 0, 0)
        keys_all = mm(x, w_pad[1], 0, 0)
        values_n = mm(x, w_pad[2], 0, 0)
        at = pl.ds(pl.multiple_of(t * piece, LANES), piece)
        for h in range(heads):
            q_t[h, t, 0:HDIM] = queries[h * LANES : h * LANES + HDIM].astype(BF16)
            q_t[h, t, HDIM:] = q_rows
            v_t[h, :, at] = values[h * LANES : h * LANES + HDIM + AUG].astype(BF16)
            k_n[h, t] = keys_all[:, h * LANES : (h + 1) * LANES].astype(BF16)
            v_n[h, t] = values_n[:, h * LANES : (h + 1) * LANES].astype(BF16)

    def project_step(i, _):
        project(me ^ i)
        return 0

    project(me)
    for d in range(1, seq):
        x_copies[d].wait_recv()
    lax.fori_loop(1, seq, project_step, 0)

    def place(i):
        return me ^ (seq - 1 - i // heads), lax.rem(i, heads)

    def score(i, scores):
        t, h = place(i)
        scores[...] = mm(k_n[h].reshape(slots, LANES), q_t[h, t], 1, 0)

    def finish(i, scores):
        t, h = place(i)
        top = jnp.max(scores[...], axis=0, keepdims=True)
        weights = jnp.exp2(scores[...] - top).astype(BF16)
        result = mm(v_t[h], weights, 1, 0)
        total = result[HDIM : HDIM + 1]
        context_s[t, pl.ds(pl.multiple_of(h * HDIM, HDIM), HDIM)] = (
            result[0:HDIM] / total
        ).astype(BF16)
        lse = top + jnp.log2(total)
        high, middle, low = three_parts(-lse)
        value = jnp.where(aug_row == 0, 1.0, 0.0)
        for r, part in enumerate((high, middle, low)):
            value = jnp.where(aug_row == r + 1, part.astype(F32), value)
        q_t[h, t, HDIM : HDIM + AUG] = value.astype(BF16)

    def c_copy(d):
        return remote(
            context_s.at[me ^ d], context_r.at[me], c_send.at[d], c_recv.at[d], seq=me ^ d
        )

    if split:

        def forward(e):
            src = lax.rem(my_dp + n_dp - e, n_dp)
            ou = gath_ou.at[xbit, src, core]
            dd = gath_d.at[src, me]
            out = []
            for sems, partner in (((x_send, x_recv), me ^ 2), ((y_send, y_recv), me ^ 1)):
                out.append(
                    remote(ou, ou, sems[0].at[e, 0], sems[1].at[e, 0], seq=partner)
                )
                out.append(
                    remote(dd, dd, sems[0].at[e, 1], sems[1].at[e, 1], seq=partner)
                )
            return out

        def onward(e):
            src = lax.rem(my_dp + n_dp - e, n_dp)
            ou = gath_ou.at[1 - xbit, src, core]
            dd = gath_d.at[src, me ^ 2]
            return [
                remote(ou, ou, z_send.at[e, 0], z_recv.at[e, 0], seq=me ^ 1),
                remote(dd, dd, z_send.at[e, 1], z_recv.at[e, 1], seq=me ^ 1),
            ]

        def do_forward(e):
            for copy in p_pair(e, ow):
                copy.wait_recv()
            for copy in forward(e):
                copy.start()

        def do_onward(e):
            for copy in forward(e)[:2]:
                copy.wait_recv()
            for copy in onward(e):
                copy.start()

    blocks = seq * heads
    last = blocks // 2 - 1

    def send_if_done(i):
        d = seq - 1 - i // heads

        @pl.when((lax.rem(i, heads) == heads - 1) & (d > 0))
        def _():
            c_copy(d).start()

    def steps(u):
        if not split:
            return
        for e in range(1, n_dp):

            @pl.when(u == 1 + e // 2)
            def _():
                do_forward(e)

            if 2 + e // 2 < last:

                @pl.when(u == 2 + e // 2)
                def _():
                    do_onward(e)

    def pair(u, _):
        steps(u)
        score(2 * u + 1, scores1)
        finish(2 * u, scores0)
        send_if_done(2 * u)
        score(2 * u + 2, scores0)
        finish(2 * u + 1, scores1)
        send_if_done(2 * u + 1)
        return 0

    score(0, scores0)
    lax.fori_loop(0, last, pair, 0)
    if split:
        for e in range(1, n_dp):
            if 1 + e // 2 >= last:
                do_forward(e)
        for e in range(1, n_dp):
            if 2 + e // 2 >= last:
                do_onward(e)
    score(2 * last + 1, scores1)
    finish(2 * last, scores0)
    finish(2 * last + 1, scores1)
    context_r[me] = context_s[me]

    for d in range(1, seq):
        c_copy(d).wait()
        x_copies[d].wait_send()
    if split:
        for e in range(1, n_dp):
            s_copies[e - 1].wait_send()
            for copy in p_pair(e, ow):
                copy.wait_send()
            for copy in forward(e)[:2]:
                copy.wait_send()
            for copy in forward(e)[2:]:
                copy.wait()
            for copy in onward(e):
                copy.wait()

        @pl.when(holder)
        def _():
            for e in range(1, n_dp):
                for kind in range(3):
                    w_copy(kind, e).wait_send()


def attend(cfg, row, collective_id, *args):
    c = cfg
    g, l, h, s = c.group, c.piece, c.heads, c.seq
    sds = jax.ShapeDtypeStruct
    out_shape = [
        sds((s, g, l), BF16),
        sds((h, s, LANES, l), BF16),
        sds((h, s, l, LANES), BF16),
        sds((h, s, l, LANES), BF16),
        sds((s, g, l), BF16),
        sds((s, g + AUG, l), BF16),
        sds((GROUPS, g, l), BF16),
        sds((3, g, g), BF16),
    ]
    if c.split:
        out_shape += [
            sds((c.dp, 16, LANES), F32),
            sds((2, c.dp, 2, c.half, c.width), BF16),
            sds((c.dp, 4, c.quarter, g), BF16),
        ]
    dma = pltpu.SemaphoreType.DMA
    scratch = [
        pltpu.VMEM((h, HDIM + AUG, c.slots), BF16),
        pltpu.VMEM((c.slots, l), F32),
        pltpu.VMEM((c.slots, l), F32),
        pltpu.VMEM((3, g + AUG, h * LANES), BF16),
        dma((s,)),
        dma((s,)),
        dma((s,)),
        dma((s,)),
    ]
    if c.split:
        scratch += [
            pltpu.VMEM((c.per_group, 3, c.shard, g), BF16),
            dma((c.dp,)),
            dma((c.dp,)),
            dma((c.dp, 3)),
            dma((c.per_group, 3)),
            dma((3,)),
        ] + [dma((c.dp, 2))] * 8
    vmem = pl.BlockSpec(memory_space=pltpu.VMEM)
    return pl.pallas_call(
        functools.partial(attend_kernel, cfg, row),
        out_shape=out_shape,
        in_specs=[vmem] * len(args),
        out_specs=[vmem] * len(out_shape),
        scratch_shapes=scratch,
        compiler_params=pltpu.CompilerParams(
            collective_id=collective_id, has_side_effects=True, vmem_limit_bytes=VMEM_LIMIT
        ),
        name="attend",
    )(*args)


def middle_kernel(
    cfg,
    row,
    context,
    x_own,
    teacher,
    out_grad,
    wo,
    wu,
    wd,
    smalls,
    cols,
    up_rows,
    layer_out,
    c_grad,
    grad_mid,
    g_ou,
    g_d,
    vecs,
    v1,
    first,
    low1,
    act,
    slope,
    v2,
    seed,
    low2,
    inner_low,
    w_up,
    vcols,
    raw,
):
    me = lax.axis_index("seq")
    my_dp = lax.axis_index("dp")
    piece, width, group = cfg.piece, cfg.width, cfg.group
    hid = cfg.hidden // GROUPS
    rows = 32
    chunks = width // rows
    inv = 1.0 / width
    total = jnp.sum(smalls[:, 12:13, 0:1], axis=0)
    for r in range(1, cfg.rows):
        total += jnp.sum(smalls[:, 12 + r : 13 + r, 0:1], axis=0)
    length = smalls[my_dp, 12 + row : 13 + row, 0:1]
    slot = (iota((1, piece), 1) + me * piece).astype(F32)
    live = jnp.where(slot < length, 1.0, 0.0)
    coef = 2.0 / (total * width)

    def at(i, n):
        return pl.ds(pl.multiple_of(i * n, n), n)

    def col(i, n, which):
        return cols[at(i, n), which : which + 1]

    def loop(count, body, *init):
        return lax.fori_loop(0, count, lambda i, c: body(i, *c), tuple(init))

    zero_row = jnp.zeros((1, piece), F32)

    def sub(v):
        return jnp.sum(v, axis=0, keepdims=True)

    for g in range(GROUPS):
        w_up[g, 0:group] = wu[g * group : (g + 1) * group]
        w_up[g, group:] = jnp.where(
            iota((AUG, hid), 0) == 0, up_rows[g : g + 1].astype(F32), 0.0
        ).astype(BF16)
        low1[g, group:] = jnp.where(iota((AUG, piece), 0) == 0, 1.0, 0.0).astype(BF16)
    vcols[...] = jnp.zeros_like(vcols)

    step = 256

    def project(i, acc):
        out = mm(wo[:, at(i, step)], context[...], 0, 0)
        v = out + x_own[at(i, step)].astype(F32) + col(i, step, 0)
        v1[at(i, step)] = v
        return (acc + sub(v),)

    (acc,) = loop(width // step, project, zero_row)
    mean = acc * inv

    def center1(i, acc):
        v = v1[at(i, rows)] - mean
        v1[at(i, rows)] = v
        return (acc + sub(v * v),)

    (acc,) = loop(chunks, center1, zero_row)
    scale1 = lax.rsqrt(acc * inv + EPSILON)
    per = group // rows

    def norm1(i, unused):
        v = v1[at(i, rows)] * scale1
        v1[at(i, rows)] = v
        out = v * col(i, rows, 1) + col(i, rows, 2)
        first[at(i, rows)] = out
        low1[i // per, at(lax.rem(i, per), rows)] = out.astype(BF16)
        return (unused,)

    loop(chunks, norm1, 0)

    parts = hid // step

    def expand(i, unused):
        g, c = i // parts, lax.rem(i, parts)
        raw[...] = mm(w_up[g, :, at(c, step)], low1[g], 0, 0)

        def gelu(k, unused):
            u = raw[at(k, rows)]
            x = jnp.abs(u) * 0.7071067811865476
            d = 1.0 + 0.3275911 * x
            t = pl.reciprocal(d, approx=True)
            t = t * (2.0 - d * t)
            bell = jnp.exp2((u * u) * (-0.5 * LOG2E))
            poly = t * (
                0.127414796
                + t * (-0.142248368 + t * (0.7107068705 + t * (-0.7265760135 + t * 0.5307027145)))
            )
            tail = poly * bell
            phi = jnp.where(u >= 0.0, 1.0 - tail, tail)
            place = pl.ds(pl.multiple_of(i * step + k * rows, rows), rows)
            act[place] = (u * phi).astype(BF16)
            slope[place] = phi + u * bell * 0.3989422804014327
            return (unused,)

        loop(step // rows, gelu, 0)
        return (unused,)

    loop(GROUPS * parts, expand, 0)

    def contract(g, acc):
        out = mm(wd[at(g, hid)], act[at(g, hid)], 0, 0)
        v = out + first[at(g, group)] + col(g, group, 3)
        v2[at(g, group)] = v
        return (acc + sub(v),)

    (acc,) = loop(GROUPS, contract, zero_row)
    mean = acc * inv

    def center2(i, acc):
        v = v2[at(i, rows)] - mean
        v2[at(i, rows)] = v
        return (acc + sub(v * v),)

    (acc,) = loop(chunks, center2, zero_row)
    scale2 = lax.rsqrt(acc * inv + EPSILON)

    loss, sum1, sum2 = zero_row, zero_row, zero_row
    for c in range(width // LANES):
        span = slice(c * LANES, (c + 1) * LANES)
        xhat = v2[span] * scale2
        v2[span] = xhat
        gain = cols[span, 4:5]
        full = xhat * gain + cols[span, 5:6]
        layer_out[:, span] = full.T.astype(BF16)
        error = full - teacher[:, span].astype(F32).T
        loss += sub(live * error * error)
        grad = live * (out_grad[:, span].astype(F32).T + error * coef)
        seed[span] = grad
        vcols[span, 4:5] = jnp.sum(grad * xhat, axis=1, keepdims=True)
        vcols[span, 5:6] = jnp.sum(grad, axis=1, keepdims=True)
        grad = grad * gain
        sum1 += sub(grad)
        sum2 += sub(grad * xhat)
    sum1, sum2 = sum1 * inv, sum2 * inv

    def back2(i, unused):
        place = at(i, rows)
        grad = scale2 * (seed[place] * col(i, rows, 4) - sum1 - v2[place] * sum2)
        seed[place] = grad
        small = grad.astype(BF16)
        low2[place] = small
        vcols[place, 3:4] = jnp.sum(small.astype(F32), axis=1, keepdims=True)
        return (unused,)

    loop(chunks, back2, 0)

    def back_act(i, unused):
        g = i // parts
        raw[...] = mm(wd[at(i, step)], low2[at(g, group)], 1, 0)
        inner_low[at(i, step)] = (raw[...] * slope[at(i, step)]).astype(BF16)
        return (unused,)

    loop(GROUPS * parts, back_act, 0)

    def back_first(g, a, b):
        place = at(g, group)
        grad = seed[place] + mm(w_up[g, 0:group], inner_low[at(g, hid)], 1, 0)
        xhat = v1[place]
        vcols[place, 1:2] = jnp.sum(grad * xhat, axis=1, keepdims=True)
        vcols[place, 2:3] = jnp.sum(grad, axis=1, keepdims=True)
        grad = grad * col(g, group, 1)
        seed[place] = grad
        return (a + sub(grad), b + sub(grad * xhat))

    sum1, sum2 = loop(GROUPS, back_first, zero_row, zero_row)
    sum1, sum2 = sum1 * inv, sum2 * inv

    def down_grad(g, unused):
        g_d[at(g, hid)] = mm(act[at(g, hid)], low2[at(g, group)], 1, 1).astype(BF16)
        return (unused,)

    loop(GROUPS, down_grad, 0)

    def back1(i, unused):
        place = at(i, rows)
        grad = scale1 * (seed[place] - sum1 - v1[place] * sum2)
        grad_mid[place] = grad
        small = grad.astype(BF16)
        low2[place] = small
        vcols[place, 0:1] = jnp.sum(small.astype(F32), axis=1, keepdims=True)
        return (unused,)

    loop(chunks, back1, 0)

    def back_context(i, unused):
        c_grad[at(i, step)] = mm(wo[at(i, step)], low2[...], 1, 0).astype(BF16)
        g_ou[0, at(i, step)] = mm(context[at(i, step)], low2[...], 1, 1).astype(BF16)
        return (unused,)

    loop(width // step, back_context, 0)

    vecs[...] = jnp.zeros_like(vecs)
    vecs[0:8] = vcols[...].T[0:8]
    for g in range(GROUPS):
        out = mm(low1[g], inner_low[g * hid : (g + 1) * hid], 1, 1)
        g_ou[1, g * group : (g + 1) * group] = out[0:group].astype(BF16)
        vecs[8 + g : 9 + g] = out[group : group + 1]
    mean_loss = jnp.sum(loss, axis=1, keepdims=True) / (total * width)
    vecs[12:13] = jnp.broadcast_to(mean_loss, (1, width))


def middle(cfg, row, *args):
    c = cfg
    sds = jax.ShapeDtypeStruct
    w, l, f = c.width, c.piece, c.hidden
    out_shape = [
        sds((l, w), BF16),
        sds((w, l), BF16),
        sds((w, l), F32),
        sds((2, w, w), BF16),
        sds((f, c.group), BF16),
        sds((16, w), F32),
    ]
    scratch = [
        pltpu.VMEM((w, l), F32),
        pltpu.VMEM((w, l), F32),
        pltpu.VMEM((GROUPS, c.group + AUG, l), BF16),
        pltpu.VMEM((f, l), BF16),
        pltpu.VMEM((f, l), F32),
        pltpu.VMEM((w, l), F32),
        pltpu.VMEM((w, l), F32),
        pltpu.VMEM((w, l), BF16),
        pltpu.VMEM((f, l), BF16),
        pltpu.VMEM((GROUPS, c.group + AUG, f // GROUPS), BF16),
        pltpu.VMEM((w, LANES), F32),
        pltpu.VMEM((256, l), F32),
    ]
    vmem = pl.BlockSpec(memory_space=pltpu.VMEM)
    return pl.pallas_call(
        functools.partial(middle_kernel, cfg, row),
        out_shape=out_shape,
        in_specs=[vmem] * len(args),
        out_specs=[vmem] * len(out_shape),
        scratch_shapes=scratch,
        compiler_params=pltpu.CompilerParams(vmem_limit_bytes=VMEM_LIMIT),
        name="middle",
    )(*args)


def backward_kernel(cfg, *refs):
    split = cfg.split
    refs = list(refs)
    take = lambda n: [refs.pop(0) for _ in range(n)]
    c_grad, q_t, k_n, v_n, context_s, x_group, w_group, grad_mid = take(8)
    if split:
        g_ou, g_d, vecs = take(3)
    states_grad, qkv_out = take(2)
    if split:
        o_out, d_out, vec_out = take(3)
    d_in, d_aug, p0, p1, s0, s1, dq, dk, dv, d_t, dx_s, dx_r = take(12)
    a_send, a_recv, x_send, x_recv = take(4)
    if split:
        r1_ou, r1_d, t1_ou, t1_d, r2_ou, r2_d, t2_ou, t2_d, r3_ou, r3_d = take(10)
        vec_in, vec_mid, vec_dp, qkv_s, qkv_r = take(5)
        r1_send, r1_recv, r2_send, r2_recv, r3_send, r3_recv, r4_send, r4_recv = take(8)
        v1_send, v1_recv, v2_send, v2_recv, w1_send, w1_recv, w2_send, w2_recv = take(8)
    me = lax.axis_index("seq")
    my_dp = lax.axis_index("dp")
    piece, width, group, heads, seq = cfg.piece, cfg.width, cfg.group, cfg.heads, cfg.seq
    n_dp, shard = cfg.dp, cfg.shard

    greet(cfg, me, my_dp, split)
    grad_copies = {}
    for d in range(1, seq):
        grad_copies[d] = remote(
            c_grad.at[me ^ d], d_in.at[me], a_send.at[d], a_recv.at[d], seq=me ^ d
        )
        grad_copies[d].start()

    if split:
        xbit, core = me // 2, lax.rem(me, 2)
        first_hop = [
            remote(g_ou.at[:, :, 1 - core], r1_ou, r1_send.at[0], r1_recv.at[0], seq=me ^ 1),
            remote(g_d.at[:, :, 1 - core], r1_d, r1_send.at[1], r1_recv.at[1], seq=me ^ 1),
        ]
        for copy in first_hop:
            copy.start()
        vec_hop = []
        for d in range(1, seq):
            vec_hop.append(
                remote(vecs, vec_in.at[me], v1_send.at[d], v1_recv.at[d], seq=me ^ d)
            )
            vec_hop[-1].start()

        second_hop = [
            remote(t1_ou.at[1 - xbit], r2_ou, r2_send.at[0], r2_recv.at[0], seq=me ^ 2),
            remote(t1_d.at[:, 1 - xbit], r2_d, r2_send.at[1], r2_recv.at[1], seq=me ^ 2),
        ]

        def third_hop(e):
            target = lax.rem(my_dp + e, n_dp)
            return [
                remote(
                    t2_ou.at[target], r3_ou.at[my_dp], r3_send.at[e, 0], r3_recv.at[e, 0], dp=target
                ),
                remote(
                    t2_d.at[target], r3_d.at[my_dp], r3_send.at[e, 1], r3_recv.at[e, 1], dp=target
                ),
            ]

        def fourth_hop(d):
            mine = o_out.at[xbit, core]
            own = d_out.at[me]
            return [
                remote(mine, mine, r4_send.at[d, 0], r4_recv.at[d, 0], seq=me ^ d),
                remote(own, own, r4_send.at[d, 1], r4_recv.at[d, 1], seq=me ^ d),
            ]

        def vec_second(e):
            return remote(
                vec_mid,
                vec_dp.at[my_dp],
                v2_send.at[e],
                v2_recv.at[e],
                dp=lax.rem(my_dp + e, n_dp),
            )

        def phase_one():
            for copy in first_hop:
                copy.wait_recv()
            for copy in vec_hop:
                copy.wait_recv()

            def add(i, _):
                for x in range(2):
                    t1_ou[x, i] = (
                        g_ou[x, i, core].astype(F32) + r1_ou[x, i].astype(F32)
                    ).astype(BF16)
                    t1_d[i, x] = (
                        g_d[i, x, core].astype(F32) + r1_d[i, x].astype(F32)
                    ).astype(BF16)
                return 0

            lax.fori_loop(0, n_dp, add, 0)
            for copy in second_hop:
                copy.start()
            value = vecs[...]
            for d in range(1, seq):
                value += vec_in[me ^ d]
            vec_mid[...] = value
            for e in range(1, n_dp):
                vec_second(e).start()

        def phase_two():
            for copy in second_hop:
                copy.wait_recv()

            def add(i, _):
                t2_ou[i] = (t1_ou[xbit, i].astype(F32) + r2_ou[i].astype(F32)).astype(BF16)
                t2_d[i] = (t1_d[i, xbit].astype(F32) + r2_d[i].astype(F32)).astype(BF16)
                return 0

            lax.fori_loop(0, n_dp, add, 0)
            for e in range(1, n_dp):
                for copy in third_hop(e):
                    copy.start()
            value = vec_mid[...]
            for e in range(1, n_dp):
                vec_second(e).wait_recv()
            for e in range(1, n_dp):
                value += vec_dp[lax.rem(my_dp + e, n_dp)]
            vec_out[...] = value

        def phase_three():
            for e in range(1, n_dp):
                for copy in third_hop(e):
                    copy.wait_recv()
            ou = t2_ou[my_dp].astype(F32)
            dd = t2_d[my_dp].astype(F32)
            for e in range(1, n_dp):
                src = lax.rem(my_dp + e, n_dp)
                ou += r3_ou[src].astype(F32)
                dd += r3_d[src].astype(F32)
            o_out[xbit, core] = ou.astype(BF16)
            d_out[me] = dd.astype(BF16)
            for d in range(1, seq):
                for copy in fourth_hop(d):
                    copy.start()

    def clear(ref):
        def body(i, _):
            ref[i] = jnp.zeros(ref.shape[1:], ref.dtype)
            return 0

        lax.fori_loop(0, ref.shape[0], body, 0)

    clear(dq)
    clear(dk)
    clear(dv)
    aug_row = iota((HDIM, piece), 0)

    def prepare(t):
        for h in range(heads):
            grad = d_in[t, h * HDIM : (h + 1) * HDIM]
            d_aug[h, t, 0:HDIM] = grad
            dot = jnp.sum(
                grad.astype(F32) * context_s[t, h * HDIM : (h + 1) * HDIM].astype(F32),
                axis=0,
                keepdims=True,
            )
            high, middle, low = three_parts(-dot)
            value = jnp.where(aug_row == 0, high.astype(F32), 0.0)
            value = jnp.where(aug_row == 1, middle.astype(F32), value)
            value = jnp.where(aug_row == 2, low.astype(F32), value)
            d_aug[h, t, HDIM:] = value.astype(BF16)

    per_piece = heads * seq
    blocks = seq * per_piece

    def place(i):
        j = lax.rem(i, per_piece)
        return me ^ (i // per_piece), j // seq, lax.rem(j, seq)

    def score(i, p, s):
        a, h, b = place(i)
        weights = jnp.exp2(mm(q_t[h, a], k_n[h, b], 0, 1))
        p[...] = weights.astype(BF16)
        s[...] = (weights * mm(d_aug[h, a], v_n[h, b], 0, 1)).astype(BF16)

    def finish(i, p, s):
        a, h, b = place(i)
        dv[h * seq + b] += mm(d_aug[h, a, 0:HDIM], p[...], 1, 0)
        dk[h * seq + b] += mm(q_t[h, a, 0:HDIM], s[...], 1, 0)
        dq[h * seq + a] += mm(s[...], k_n[h, b], 1, 0)

    d_in[me] = c_grad[me]
    prepare(me)
    steps_piece = per_piece // 2

    def pair(u, _):
        for d in range(1, seq):

            @pl.when(u == d * steps_piece - 1)
            def _():
                grad_copies[d].wait_recv()
                prepare(me ^ d)

        if split:
            pl.when(u == 2)(phase_one)
            pl.when(u == 9)(phase_two)
            pl.when(u == 16)(phase_three)
        score(2 * u + 1, p1, s1)
        finish(2 * u, p0, s0)
        score(2 * u + 2, p0, s0)
        finish(2 * u + 1, p1, s1)
        return 0

    score(0, p0, s0)
    last = blocks // 2 - 1
    lax.fori_loop(0, last, pair, 0)
    score(2 * last + 1, p1, s1)
    finish(2 * last, p0, s0)
    finish(2 * last + 1, p1, s1)

    def collect(t):
        for h in range(heads):
            at = slice(h * HDIM, (h + 1) * HDIM)
            d_t[t, 0, at] = (dq[h * seq + t] * HDIM**-0.5).T[0:HDIM].astype(BF16)
            d_t[t, 1, at] = (dk[h * seq + t] * (1.0 / LOG2E)).astype(BF16)
            d_t[t, 2, at] = dv[h * seq + t].astype(BF16)
        out = mm(w_group[0], d_t[t, 0], 1, 0)
        out += mm(w_group[1], d_t[t, 1], 1, 0)
        out += mm(w_group[2], d_t[t, 2], 1, 0)
        dx_s[t] = out.astype(BF16)

    def slab(t):
        return dx_r.at[pl.ds(pl.multiple_of(t * group, HDIM), group)]

    def dx_copy(d):
        return remote(dx_s.at[me ^ d], slab(me), x_send.at[d], x_recv.at[d], seq=me ^ d)

    def collect_step(i, _):
        collect(me ^ (seq - 1 - i))
        for d in range(1, seq):

            @pl.when(i == seq - 1 - d)
            def _():
                dx_copy(d).start()

        return 0

    lax.fori_loop(0, seq, collect_step, 0)
    for kind in range(3):
        total = mm(x_group[0], d_t[0, kind], 1, 1)
        for t in range(1, seq):
            total += mm(x_group[t], d_t[t, kind], 1, 1)
        if split:
            for t in range(cfg.per_group):
                qkv_s[t, kind, 0:shard] = total[t * shard : (t + 1) * shard].astype(BF16)
                qkv_s[t, kind, shard:] = total[group:].astype(BF16)
        else:
            qkv_out[kind] = total
    dx_r[pl.ds(pl.multiple_of(me * group, HDIM), group)] = dx_s[me]

    if split:
        my_slot = lax.rem(my_dp, cfg.per_group)
        owner_seq = my_dp // cfg.per_group
        owner = owner_seq == me

        def w_first(t):
            return remote(
                qkv_s.at[t],
                qkv_r.at[my_dp],
                w1_send.at[t],
                w1_recv.at[my_dp],
                dp=me * cfg.per_group + t,
            )

        for t in range(cfg.per_group):

            @pl.when(me * cfg.per_group + t != my_dp)
            def _():
                w_first(t).start()

        def w_second(d):
            return remote(qkv_out, qkv_out, w2_send.at[d], w2_recv.at[0], seq=me ^ d)

        @pl.when(owner)
        def _():
            total = qkv_s[my_slot].astype(F32)
            for e in range(1, n_dp):
                src = lax.rem(my_dp + e, n_dp)
                remote(
                    qkv_s.at[0], qkv_r.at[src], w1_send.at[0], w1_recv.at[src], dp=src
                ).wait_recv()
                total += qkv_r[src].astype(F32)
            qkv_out[...] = total.astype(BF16)
            for d in range(1, seq):
                w_second(d).start()

    for d in range(1, seq):
        dx_copy(d).wait_recv()
    for c in range(width // LANES):
        span = slice(c * LANES, (c + 1) * LANES)
        states_grad[:, span] = (dx_r[span].astype(F32) + grad_mid[span]).T.astype(BF16)

    for d in range(1, seq):
        dx_copy(d).wait_send()
        grad_copies[d].wait_send()
    if split:
        for t in range(cfg.per_group):

            @pl.when(me * cfg.per_group + t != my_dp)
            def _():
                w_first(t).wait_send()

        @pl.when(owner)
        def _():
            for d in range(1, seq):
                w_second(d).wait_send()

        @pl.when(jnp.logical_not(owner))
        def _():
            w_second(1).wait_recv()

        for copy in first_hop + second_hop + vec_hop:
            copy.wait_send()
        for e in range(1, n_dp):
            vec_second(e).wait_send()
            for copy in third_hop(e):
                copy.wait_send()
        for d in range(1, seq):
            for copy in fourth_hop(d):
                copy.wait()


def backward(cfg, collective_id, *args):
    c = cfg
    sds = jax.ShapeDtypeStruct
    g, l, h, s, w = c.group, c.piece, c.heads, c.seq, c.width
    if c.split:
        out_shape = [
            sds((l, w), BF16),
            sds((3, c.shard + AUG, g), BF16),
            sds((2, 2, c.half, w), BF16),
            sds((4, c.quarter, g), BF16),
            sds((16, w), F32),
        ]
    else:
        out_shape = [sds((l, w), BF16), sds((3, g + AUG, g), F32)]
    dma = pltpu.SemaphoreType.DMA
    vm = pltpu.VMEM
    scratch = [
        vm((s, g, l), BF16),
        vm((h, s, LANES, l), BF16),
        vm((l, l), BF16),
        vm((l, l), BF16),
        vm((l, l), BF16),
        vm((l, l), BF16),
        vm((h * s, l, LANES), F32),
        vm((h * s, HDIM, l), F32),
        vm((h * s, HDIM, l), F32),
        vm((s, 3, g, l), BF16),
        vm((s, g, l), BF16),
        vm((w, l), BF16),
        dma((s,)),
        dma((s,)),
        dma((s,)),
        dma((s,)),
    ]
    if c.split:
        ou = (c.half, w)
        dd = (c.quarter, g)
        scratch += [
            vm((2, c.dp) + ou, BF16),
            vm((c.dp, 2) + dd, BF16),
            vm((2, c.dp) + ou, BF16),
            vm((c.dp, 2) + dd, BF16),
            vm((c.dp,) + ou, BF16),
            vm((c.dp,) + dd, BF16),
            vm((c.dp,) + ou, BF16),
            vm((c.dp,) + dd, BF16),
            vm((c.dp,) + ou, BF16),
            vm((c.dp,) + dd, BF16),
            vm((s, 16, w), F32),
            vm((16, w), F32),
            vm((c.dp, 16, w), F32),
            vm((c.per_group, 3, c.shard + AUG, g), BF16),
            vm((c.dp, 3, c.shard + AUG, g), BF16),
            dma((2,)),
            dma((2,)),
            dma((2,)),
            dma((2,)),
            dma((c.dp, 2)),
            dma((c.dp, 2)),
            dma((s, 2)),
            dma((s, 2)),
            dma((s,)),
            dma((s,)),
            dma((c.dp,)),
            dma((c.dp,)),
            dma((c.per_group,)),
            dma((c.dp,)),
            dma((s,)),
            dma((1,)),
        ]
    vmem = pl.BlockSpec(memory_space=pltpu.VMEM)
    return pl.pallas_call(
        functools.partial(backward_kernel, cfg),
        out_shape=out_shape,
        in_specs=[vmem] * len(args),
        out_specs=[vmem] * len(out_shape),
        scratch_shapes=scratch,
        compiler_params=pltpu.CompilerParams(
            collective_id=collective_id, has_side_effects=True, vmem_limit_bytes=VMEM_LIMIT
        ),
        name="backward",
    )(*args)


def local(
    states,
    lengths,
    teacher,
    out_grad,
    q_weight,
    k_weight,
    v_weight,
    q_bias,
    v_bias,
    o_weight,
    o_bias,
    attn_gain,
    attn_bias,
    up_weight,
    up_bias,
    down_weight,
    down_bias,
    ffn_gain,
    ffn_bias,
):
    row_count, piece, width = states.shape
    n_dp, n_seq = lax.axis_size("dp"), lax.axis_size("seq")
    me, my_dp = lax.axis_index("seq"), lax.axis_index("dp")
    shard = q_bias.shape[0]
    hidden = up_bias.shape[0] * n_dp
    cfg = Config(n_dp, n_seq, piece, width, hidden, shard)
    cfg.rows = row_count
    group = cfg.group

    def pad(v):
        return jnp.pad(v.astype(F32), ((0, 0), (0, LANES - v.shape[1])))

    vectors = (q_bias, v_bias, o_bias, attn_gain, attn_bias, down_bias, ffn_gain, ffn_bias)
    small = jnp.concatenate(
        [
            pad(jnp.stack(vectors)),
            pad(up_bias.reshape(4, shard)),
            jnp.broadcast_to(lengths.astype(F32)[:, None], (row_count, LANES)),
            jnp.zeros((4 - row_count, LANES), F32),
        ]
    )
    if not cfg.split:
        smalls = lax.all_gather(small, "dp", axis=0)
        qkv = jnp.stack((q_weight, k_weight, v_weight))
        qkv = lax.all_gather(qkv, "dp", axis=1, tiled=True)
        w_group_in = lax.dynamic_slice(qkv, (0, me * group, 0), (3, group, group))
        wo = lax.all_gather(o_weight, "dp", axis=0, tiled=True)
        wu = lax.all_gather(up_weight, "dp", axis=0, tiled=True)
        wd = lax.all_gather(down_weight, "dp", axis=0, tiled=True)

    results = []
    for r in range(row_count):
        if cfg.split:
            (
                context_r,
                q_t,
                k_n,
                v_n,
                context_s,
                x_group,
                x_own,
                w_group,
                smalls,
                gath_ou,
                gath_d,
            ) = attend(
                cfg,
                r,
                2 * r,
                states[r],
                small,
                q_weight,
                k_weight,
                v_weight,
                o_weight,
                up_weight,
                down_weight,
            )
            gath_ou = gath_ou.reshape(2, width, width)
            wo, wu = gath_ou[0], gath_ou[1]
            wd = gath_d.reshape(hidden, group)
        else:
            context_r, q_t, k_n, v_n, context_s, x_group, x_own, w_group = attend(
                cfg, r, 2 * r, states[r], smalls, w_group_in
            )
        cols = smalls[:, 2:8, :shard].transpose(0, 2, 1).reshape(width, 6)
        cols = jnp.pad(cols, ((0, 0), (0, LANES - 6)))
        up_rows = smalls[:, 8:12, :shard].reshape(GROUPS, hidden // GROUPS)
        layer_out, c_grad, grad_mid, g_ou, g_d, vecs = middle(
            cfg,
            r,
            context_r.reshape(width, piece),
            x_own.reshape(width, piece),
            teacher[r],
            out_grad[r],
            wo,
            wu,
            wd,
            smalls,
            cols,
            up_rows,
        )
        c_grad = c_grad.reshape(GROUPS, group, piece)
        common = (c_grad, q_t, k_n, v_n, context_s, x_group, w_group, grad_mid)
        if cfg.split:
            g_ou = g_ou.reshape(2, n_dp, 2, cfg.half, width)
            g_d = g_d.reshape(n_dp, 2, 2, cfg.quarter, group)
            states_grad, qkv, ou, dd, vec = backward(cfg, 2 * r + 1, *common, g_ou, g_d, vecs)
            ou = ou.reshape(2, shard, width).astype(F32)
            grads = (
                qkv[:, :shard].astype(F32),
                qkv[:, shard].astype(F32),
                ou,
                dd.reshape(4 * shard, group).astype(F32),
                vec,
            )
        else:
            states_grad, qkv = backward(cfg, 2 * r + 1, *common)
            grads = (qkv, g_ou.astype(F32), g_d.astype(F32), vecs)
        results.append((layer_out, states_grad, grads))

    layer_out = jnp.stack([item[0] for item in results])
    states_grad = jnp.stack([item[1] for item in results])
    grads = jax.tree.map(lambda *leaves: sum(leaves[1:], leaves[0]), *[i[2] for i in results])
    if cfg.split:
        qkv, qkv_bias, ou, grad_dw, vec = grads
        at = lax.rem(my_dp, cfg.per_group) * shard
        grad_qb = lax.dynamic_slice(qkv_bias[0], (at,), (shard,))
        grad_vb = lax.dynamic_slice(qkv_bias[2], (at,), (shard,))
        grad_ow, grad_uw = ou[0], ou[1]
    else:
        qkv_g, g_ou, g_d, vecs = grads
        whole = jnp.zeros((3, width + GROUPS * AUG, group), F32)
        whole = lax.dynamic_update_slice(whole, qkv_g[:, :group], (0, me * group, 0))
        whole = lax.dynamic_update_slice(whole, qkv_g[:, group:], (0, width + me * AUG, 0))
        whole, g_ou, g_d, vec = lax.psum((whole, g_ou, g_d, vecs), ("dp", "seq"))
        qkv = lax.dynamic_slice(whole, (0, my_dp * shard, 0), (3, shard, group))
        biases = whole[:, width::AUG].reshape(3, width)
        grad_qb = lax.dynamic_slice(biases[0], (my_dp * shard,), (shard,))
        grad_vb = lax.dynamic_slice(biases[2], (my_dp * shard,), (shard,))
        g_ou = lax.dynamic_slice(g_ou, (0, my_dp * shard, 0), (2, shard, width))
        grad_ow, grad_uw = g_ou[0], g_ou[1]
        grad_dw = lax.dynamic_slice(g_d, (my_dp * 4 * shard, 0), (4 * shard, group))

    mine = lax.dynamic_slice(vec[:6], (0, my_dp * shard), (6, shard))
    grad_ub = lax.dynamic_slice(vec[8:12].reshape(-1), (my_dp * 4 * shard,), (4 * shard,))
    return (
        layer_out,
        vec[12, 0],
        states_grad,
        qkv[0],
        qkv[1],
        qkv[2],
        grad_qb,
        grad_vb,
        grad_ow,
        mine[0],
        mine[1],
        mine[2],
        grad_uw,
        grad_ub,
        grad_dw,
        mine[3],
        mine[4],
        mine[5],
    )


def solution(mesh):
    rows3 = P("dp", "seq", None)
    matrix = P("dp", None)
    vector = P("dp")
    return jax.shard_map(
        local,
        mesh=mesh,
        in_specs=(rows3, vector, rows3, rows3)
        + (matrix,) * 3
        + (vector,) * 2
        + (matrix,)
        + (vector,) * 3
        + (matrix, vector, matrix)
        + (vector,) * 3,
        out_specs=(rows3, P(), rows3)
        + (matrix,) * 3
        + (vector,) * 2
        + (matrix,)
        + (vector,) * 3
        + (matrix, vector, matrix)
        + (vector,) * 3,
        check_vma=False,
    )
```

time: 1260 us -> 252 us (0.20)
  waiting for transfers between devices: 400 us -> 0 us
  blocking collectives: 291 us -> 0 us
  Pallas kernels: 0 us -> 228 us
  matrix products: 195 us -> 0 us
  local copies, waits for them, and re-layouts: 181 us -> 16.5 us
  other arithmetic: 127 us -> 2.46 us
  starting transfers between devices: 31.7 us -> 0 us
  between operations: 20.5 us -> 1.38 us
    reduce_scatter x6 -> x0, waiting for transfers between devices: 288 us -> none  [the longest x1 72.5 us: local(): lax.psum_scatter(summed[9], 'dp', scatter_dimension=0, tiled=True)]
    pallas_call x0 -> x3, Pallas kernels: none -> 228 us  [the longest x1 102 us: backward(): pl.pallas_call(functools.partial(backward_kernel, cfg), out_shape=out_sha...]
    dot_general x123 -> x0, matrix products: 195 us -> none  [the longest x30 39 us: block_step(): jnp.einsum('qd,kd->qk', query_block, keys_all, preferred_element_type=jnp...]
    all_gather x4 -> x0, blocking collectives: 120 us -> none  [the longest x1 31.3 us: local(): lax.all_gather(q_weight, 'dp', axis=0, tiled=True)]
    psum x3 -> x0, blocking collectives: 95.7 us -> none  [the longest x2 84.4 us: local(): err_total, live_total = lax.psum((err_sum, live_sum), ('dp', 'seq'))]
    psum x1 -> x0, waiting for transfers between devices: 94.9 us -> none  [local(): lax.psum(partial_grads[0].astype(jnp.bfloat16), 'seq').astype(jnp.float32)]
    unnamed x2 -> x0, blocking collectives: 76 us -> none
    unnamed x143 -> x9, local copies, waits for them, and re-layouts: 71.6 us -> 3.55 us
  transfers between devices with their start and end apart: 18 -> 0, of which waited for: 8 -> 0; matrix products, arithmetic and copies ran while one was open for 20% -> 0% of each run, Pallas kernels for 0% -> 0%
where the time goes in v1:
time: 252 us; the launch traced here: 249 us
  Pallas kernels  228 us (90%)
  local copies, waits for them, and re-layouts  16.5 us (7%)
    pallas_call x1, Pallas kernels, backward(): pl.pallas_call(functools.partial(backward_kernel, cfg), out_shape=out_sha...  102 us
    pallas_call x1, Pallas kernels, attend(): pl.pallas_call(functools.partial(attend_kernel, cfg, row), out_shape=out_...  81.8 us
    pallas_call x1, Pallas kernels, middle(): pl.pallas_call(functools.partial(middle_kernel, cfg, row), out_shape=out_...  43.9 us

profile of v1, /device:TPU:0, one launch (start us, length us, event | category | flops | bytes accessed | tf_op | source)
XLA Modules:
  0.0 248.6 jit_solution(8115142203593479538)
XLA Ops:
  0.7 1.7 copy.37.refs_7_
  2.4 0.8 stack.41
  3.2 0.8 convert_element_type.31
  4.7 0.1 pad.26.clone
  4.8 0.7 maximum_maximum_fusion.refs_1_
  5.4 81.8 %attend.1 = (bf16[4,192,640]{2,1,0:T(8,128)(2,1)}, bf16[3,4,128,640]{3,2,1,0:T(8,128)(2,1)}, bf16[3,4,640,128]{3,2,1,0:T(8,128)(2,1)}, bf16[3,4,640,128]{3,2,1,0...) custom-call(bf16[640,768]{1,0:T(8,128)(2,1)} %bitcast.59, ...), custom_call_target="tpu_custom_call" | custom-call | tf_op jit(solution)/shard_map/attend/pallas_call | solution.py:472
  87.3 0.8 slice_bitcast_fusion.3
  88.0 0.2 copy.38
  88.2 0.8 pad.22.cols
  89.0 0.8 slice.75
  89.8 0.7 reshape.96.up_rows
  90.5 3.1 %fusion.2 = (bf16[1,8,2,48,768]{4,3,2,1,0:T(8,128)(2,1)}, bf16[1,8,2,48,768]{4,3,2,1,0:T(8,128)(2,1)}) fusion(bf16[2,8,2,48,768]{4,3,2,1,0:T(8,128)(2,1)} %get-tuple-element.42), kind=kLoop, calls=%fused_computation.21 | loop fusion | bytes 4718592 | tf_op jit(solution)/shard_map/slice | solution.py:1244
  93.6 43.9 %middle.1 = (bf16[640,768]{1,0:T(8,128)(2,1)}, bf16[768,640]{1,0:T(8,128)(2,1)}, f32[768,640]{1,0:T(8,128)}, bf16[2,768,768]{2,1,0:T(8,128)(2,1)}, bf16[3072,192]{1,0:T(8,128)(2,1)}, /*index=5*/f32[16,768]{1,0:T(8,128)}) custom-call(bf16[768,640]{1,0:T(8,128)(2,1)} %bitcast.63, bf16[768,640]{1,0:T(8,128)(2,1)} %bitcast.64, bf16[640,768]{1,0:T(8,128)(2,1)} %bitcast.60, ...), custom_call_target="tpu_custom_call" | custom-call | tf_op jit(solution)/shard_map/middle/pallas_call | solution.py:742
  137.5 102.5 %backward.1 = (bf16[640,768]{1,0:T(8,128)(2,1)}, bf16[3,112,192]{2,1,0:T(8,128)(2,1)}, bf16[2,2,48,768]{3,2,1,0:T(8,128)(2,1)}, bf16[4,96,192]{2,1,0:T(8,128)(2,1)}, f32[16,768]{1,0:T(8,128)}) custom-call(bf16[4,192,640]{2,1,0:T(8,128)(2,1)} %bitcast.65, bf16[3,4,128,640]{3,2,1,0:T(8,128)(2,1)} %get-tuple-element.47.refs_1_, ...), custom_call_target="tpu_custom_call" | custom-call | tf_op jit(solution)/shard_map/backward/pallas_call | solution.py:1151
  240.0 0.8 slice_convert_fusion.1
  240.9 0.6 fusion
  241.4 1.0 bitcast_convert_fusion
  242.4 0.9 copy.39
  243.3 1.8 fusion.3
  245.1 0.7 slice_bitcast_fusion
  245.9 0.5 slice_bitcast_fusion.4
  246.5 0.7 dynamic_slice.21
  247.1 0.5 slice.76
  247.6 0.9 copy.42
  (16 shorter events, 0.2 us)
Async XLA Ops:
  240.0 5.1 %copy-start.1 = (bf16[3,112,192]{2,1,0:T(8,128)(2,1)S(1)}, bf16[3,112,192]{2,1,0:T(8,128)(2,1)}, u32[]{:S(2)}) copy-start(bf16[3,112,192]{2,1,0:T(8,128)(2,1)} %get-tuple-element.59) | copy-start | bytes 387076
  240.0 5.8 %copy-start.2 = (f32[16,768]{1,0:T(8,128)S(1)}, f32[16,768]{1,0:T(8,128)}, u32[]{:S(2)}) copy-start(f32[16,768]{1,0:T(8,128)} %get-tuple-element.57) | copy-start | bytes 147460
  240.0 7.6 %copy-start = (bf16[640,768]{1,0:T(8,128)(2,1)S(1)}, bf16[640,768]{1,0:T(8,128)(2,1)}, u32[]{:S(2)}) copy-start(bf16[640,768]{1,0:T(8,128)(2,1)} %get-tuple-element.58) | copy-start | bytes 2949124
